TPU v7x, 256 devices: a whole 4x4x8 slice. The times are simulated.
256 devices in a mesh: cell: 8 (over z_lo, x), conf: 32 (over y, z_hi, core).
Axes of the slice: x: 4, y: 4, z: 8 (z_hi: 4, z_lo: 2; z = z_hi * 2 + z_lo), core: 2. Of those that a mesh axis runs over, the one named last changes fastest.
Arguments:
- density: float32 [32, 32, 32, 4096], P('conf', None, None, 'cell'), may hold values from 0 to 8, as said below
- velocity: float32 [2, 16, 256], P(None, 'cell'), may hold values from -12 to 12
- short_stress: float32 [3, 4096], P(None, ('cell', 'conf')), may hold values from -6 to 6
Outputs:
- density_next: float32 [32, 32, 32, 4096], P('conf', None, None, 'cell')
- short_next: float32 [3, 4096], P(None, ('cell', 'conf'))
- total_stress: float32 [3, 4096], P(None, ('cell', 'conf'))
Inputs may be any that keep to these rules, and one draw needn't show every extreme that they name: Each cell's configuration density is positive.
All inputs are finite; a program needn't handle non-finite values.
Results may differ from a plain program's by a relative error of at most 0.00012.
Values sent between devices are 32-bit elements; how exact they have to be, the bound alone decides.
A program may use at most 192 MiB of HBM per device.

v0:
```python
import jax
import jax.numpy as jnp
from jax import lax
from jax.sharding import PartitionSpec as P

STEPS = 2


half_extent = 3.0
fene_limit = 50.0
diffusion = 0.5
time_step = 0.001
polymer_eta = 1.0
solvent_eta = 0.5
short_relax = 0.01


def extended(array, sides, width):
    for axis, dim in sides:
        peers, length = (lax.axis_size(axis), array.shape[dim])
        up = [(i, (i + 1) % peers) for i in range(peers)]
        down = [(j, i) for i, j in up]
        last = lax.slice_in_dim(array, length - width, length, axis=dim)
        initial = lax.slice_in_dim(array, 0, width, axis=dim)
        before = lax.ppermute(last, axis, up)
        after = lax.ppermute(initial, axis, down)
        array = jnp.concatenate([before, array, after], axis=dim)
    return array


def spectral_matrix(points):
    offsets = jnp.arange(points)[:, None] - jnp.arange(points)[None, :]
    phase_angle = offsets.astype(jnp.float32) * (jnp.pi / points)
    sine_value = jnp.where(offsets == 0, jnp.float32(1.0), jnp.sin(phase_angle))
    parity = jnp.where(offsets % 2 == 0, 1.0, -1.0).astype(jnp.float32)
    entries = parity * jnp.cos(phase_angle) / sine_value * (jnp.pi / (2.0 * half_extent))
    return jnp.where(offsets == 0, jnp.float32(0.0), entries)


def grid_points(points):
    return -half_extent + (jnp.arange(points, dtype=jnp.float32) + 0.5) * (
        2.0 * half_extent / points
    )


def derive(values, which_axis, diff_matrix):
    patterns = ("jk,kabc->jabc", "jk,akbc->ajbc", "jk,abkc->abjc")
    return jnp.einsum(patterns[which_axis], diff_matrix, values, precision=lax.Precision.HIGHEST)


def drifts(coord_first, coords, gradient):
    coord_a = coord_first[:, None, None, None]
    coord_b = coords[None, :, None, None]
    coord_c = coords[None, None, :, None]
    spring = 1.0 / (1.0 - (coord_a * coord_a + coord_b * coord_b + coord_c * coord_c) / fene_limit)
    drift_a = gradient[0] * coord_a + gradient[1] * coord_b - diffusion * spring * coord_a
    drift_b = gradient[2] * coord_a + gradient[3] * coord_b - diffusion * spring * coord_b
    drift_c = -diffusion * spring * coord_c
    return (drift_a, drift_b, drift_c)


def moment_weights(coord_first, coords):
    points = coords.shape[0]
    coord_a = coord_first[:, None, None]
    coord_b = coords[None, :, None]
    coord_c = coords[None, None, :]
    spring = 1.0 / (1.0 - (coord_a * coord_a + coord_b * coord_b + coord_c * coord_c) / fene_limit)
    scale = 1.0 / float(points**3)
    stacked = jnp.stack(
        [
            coord_a * coord_a * spring,
            coord_a * coord_b * spring,
            coord_b * coord_b * spring,
            jnp.ones_like(spring),
        ]
    )
    return (stacked * scale).reshape(4, -1)


def relax(stress, gradient):
    stress_xx, stress_xy, stress_yy = (stress[0], stress[1], stress[2])
    for turn_index in range(STEPS):
        next_xx = stress_xx + time_step * (
            2.0 * (gradient[0] * stress_xx + gradient[1] * stress_xy)
            - (stress_xx - 2.0 * solvent_eta * gradient[0]) / short_relax
        )
        next_xy = stress_xy + time_step * (
            gradient[0] * stress_xy
            + gradient[1] * stress_yy
            + gradient[2] * stress_xx
            + gradient[3] * stress_xy
            - (stress_xy - solvent_eta * (gradient[1] + gradient[2])) / short_relax
        )
        next_yy = stress_yy + time_step * (
            2.0 * (gradient[2] * stress_xy + gradient[3] * stress_yy)
            - (stress_yy - 2.0 * solvent_eta * gradient[3]) / short_relax
        )
        stress_xx, stress_xy, stress_yy = (next_xx, next_xy, next_yy)
    return jnp.stack([stress_xx, stress_xy, stress_yy])


def combine_stress(moments, short_next):
    polymer = jnp.stack(
        [
            polymer_eta * (moments[0] - moments[3]),
            polymer_eta * moments[1],
            polymer_eta * (moments[2] - moments[3]),
        ]
    )
    return polymer + short_next


def on_device(density, velocity, short_stress):
    planes = density.shape[0]
    points = density.shape[1]
    cell_count = density.shape[3]
    groups = lax.axis_size("conf")
    conf_index = lax.axis_index("conf")
    block_size = cell_count // groups
    diff_matrix = spectral_matrix(points)
    coords = grid_points(points)
    padded = extended(velocity, (("cell", 1),), 1)
    grad_x = (jnp.roll(velocity, -1, 2) - jnp.roll(velocity, 1, 2)) * 0.5
    grad_y = (padded[:, 2:, :] - padded[:, :-2, :]) * 0.5
    gradient = jnp.stack([grad_x[0], grad_y[0], grad_x[1], grad_y[1]]).reshape(4, cell_count)
    own_gradient = lax.dynamic_slice_in_dim(gradient, conf_index * block_size, block_size, 1)
    short_next = relax(short_stress, own_gradient)
    coord_first = lax.dynamic_slice_in_dim(coords, conf_index * planes, planes, 0)
    drift_a, drift_b, drift_c = drifts(coord_first, coords, gradient)
    current = density
    for turn_index in range(STEPS):
        density_in = lax.all_to_all(current, "conf", split_axis=1, concat_axis=0, tiled=True)
        carried = lax.all_to_all(drift_a * current, "conf", split_axis=1, concat_axis=0, tiled=True)
        along_flux_term = carried - diffusion * derive(density_in, 0, diff_matrix)
        change = lax.all_to_all(
            derive(along_flux_term, 0, diff_matrix), "conf", split_axis=0, concat_axis=1, tiled=True
        )
        for which_axis, drift_term in ((1, drift_b), (2, drift_c)):
            flux_term = drift_term * current - diffusion * derive(current, which_axis, diff_matrix)
            change = change + derive(flux_term, which_axis, diff_matrix)
        current = current - time_step * change
    weights = moment_weights(coord_first, coords)
    partial_moments = jnp.dot(
        weights,
        current.reshape(planes * points * points, cell_count),
        precision=lax.Precision.HIGHEST,
        preferred_element_type=jnp.float32,
    )
    moments = lax.psum_scatter(partial_moments, "conf", scatter_dimension=1, tiled=True)
    return (current, short_next, combine_stress(moments, short_next))


def solution(mesh):
    return jax.shard_map(
        on_device,
        mesh=mesh,
        in_specs=(P("conf", None, None, "cell"), P(None, "cell", None), P(None, ("cell", "conf"))),
        out_specs=(
            P("conf", None, None, "cell"),
            P(None, ("cell", "conf")),
            P(None, ("cell", "conf")),
        ),
        check_vma=False,
    )
```

profile of v0, /device:TPU:1, one launch (start us, length us, event | category | flops | bytes accessed | tf_op | source)
XLA Modules:
  0.0 504.9 jit_solution(6705678125648098821)
XLA Ops:
  7.2 13.0 %all-to-all-start.1 = ((f32[1,32,32,512]{3,2,0,1:T(8,128)}), f32[1,32,32,512]{3,2,0,1:T(8,128)}, u32[]{:S(2)}, u32[]{:S(2)}) async-start(f32[1,32,32,512]{3,2,0,1:T(8,128)} %bitcast.172), calls=%async_computation.1 | async-start | bytes 4194304 | tf_op jit(solution)/shard_map/all_to_all | solution.py:132
  27.5 33.7 %collective-permute-done = f32[2,1,256]{2,1,0:T(1,128)S(1)} collective-permute-done((f32[2,1,256]{2,1,0:T(1,128)S(1)}, f32[2,1,256]{2,1,0:T(1,128)S(1)}, u32[]{:S(2)}, u32[]{:S(2)}) %collective-permute-start) | collective-permute-done | bytes 2080 | tf_op jit(solution)/shard_map/ppermute | solution.py:26
  61.2 5.8 %collective-permute-done.1 = f32[2,1,256]{2,1,0:T(1,128)S(1)} collective-permute-done((f32[2,1,256]{2,1,0:T(1,128)S(1)}, f32[2,1,256]{2,1,0:T(1,128)S(1)}, u32[]{:S(2)}, u32[]{:S(2)}) %collective-permute-start.1) | collective-permute-done | bytes 2080 | tf_op jit(solution)/shard_map/ppermute | solution.py:25
  70.9 12.5 %all-to-all-start = ((f32[1,32,32,512]{3,2,0,1:T(8,128)}), f32[1,32,32,512]{3,2,0,1:T(8,128)}, u32[]{:S(2)}, u32[]{:S(2)}) async-start(f32[1,32,32,512]{3,2,0,1:T(8,128)} %copy.44), calls=%async_computation | async-start | bytes 4194304 | tf_op jit(solution)/shard_map/all_to_all | solution.py:133
  83.4 5.9 %fusion.25 = f32[32,32,512]{2,0,1:T(8,128)} fusion(f32[1,32,32,512]{3,2,0,1:T(8,128)} %all-to-all-done.1), kind=kOutput, calls=%fused_computation.32 | convolution fusion | flops 201349120 | bytes 4194304 | tf_op jit(solution)/shard_map/jk,kabc->jabc/dot_general | solution.py:48
  89.4 44.0 %all-to-all-done = f32[1,32,32,512]{3,2,0,1:T(8,128)} async-done(((f32[1,32,32,512]{3,2,0,1:T(8,128)}), f32[1,32,32,512]{3,2,0,1:T(8,128)}, u32[]{:S(2)}, u32[]{:S(2)}) %all-to-all-start) | async-done | bytes 2097184 | tf_op jit(solution)/shard_map/all_to_all | solution.py:133
  133.4 5.3 %fusion.48 = f32[32,1,32,512]{3,0,2,1:T(8,128)S(1)} fusion(f32[1,32,32,512]{3,2,0,1:T(8,128)} %all-to-all-done, f32[32,32,512]{2,0,1:T(8,128)} %fusion.25), kind=kOutput, calls=%fused_computation.53 | convolution fusion | flops 202397696 | bytes 6291456 | tf_op jit(solution)/shard_map/jk,kabc->jabc/dot_general | solution.py:48
  141.3 6.7 %all-to-all-start.2 = ((f32[32,1,32,512]{3,2,1,0:T(8,128)}), f32[32,1,32,512]{3,2,1,0:T(8,128)}, u32[]{:S(2)}, u32[]{:S(2)}) async-start(f32[32,1,32,512]{3,2,1,0:T(8,128)} %copy.48), calls=%async_computation.2 | async-start | bytes 4194304 | tf_op jit(solution)/shard_map/all_to_all | solution.py:135
  150.0 4.4 fusion.32
  158.1 41.7 %all-to-all-done.2 = f32[32,1,32,512]{3,2,1,0:T(8,128)} async-done(((f32[32,1,32,512]{3,2,1,0:T(8,128)}), f32[32,1,32,512]{3,2,1,0:T(8,128)}, u32[]{:S(2)}, u32[]{:S(2)}) %all-to-all-start.2) | async-done | bytes 2097184 | tf_op jit(solution)/shard_map/all_to_all | solution.py:135
  199.8 11.8 %subtract_multiply_fusion.2 = (f32[1,32,32,512]{3,1,2,0:T(8,128)}, f32[1,32,32,512]{3,1,2,0:T(8,128)S(1)}) fusion(f32[32,32]{0,1:T(8,128)S(1)} %copy.42, f32[32,512]{1,0:T(8,128)S(1)} %get-tuple-element.43, f32[32,512,32]{1,2,0:T(8,128)} %fusion.17, f32[32,32,512]{2,0,1:T(8,128)} %fusion.32, f32[1,32,32,512]{3,2,1,0:T(8,128)S(1)} %copy-done, ...), kind=kOutput, calls=%fused_computation.2 | convolution fusion | flops 206592000 | bytes 12722176 | tf_op jit(solution)/shard_map/jk,akbc->ajbc/dot_general | solution.py:48
  215.5 5.7 %all-to-all-start.4 = ((f32[1,32,32,512]{3,2,0,1:T(8,128)}), f32[1,32,32,512]{3,2,0,1:T(8,128)}, u32[]{:S(2)}, u32[]{:S(2)}) async-start(f32[1,32,32,512]{3,2,0,1:T(8,128)} %copy.57), calls=%async_computation.4 | async-start | bytes 4194304 | tf_op jit(solution)/shard_map/all_to_all | solution.py:132
  223.8 48.9 %all-to-all-done.4 = f32[1,32,32,512]{3,2,0,1:T(8,128)} async-done(((f32[1,32,32,512]{3,2,0,1:T(8,128)}), f32[1,32,32,512]{3,2,0,1:T(8,128)}, u32[]{:S(2)}, u32[]{:S(2)}) %all-to-all-start.4) | async-done | bytes 2097184 | tf_op jit(solution)/shard_map/all_to_all | solution.py:132
  272.7 4.8 all-to-all-start.3
  277.5 5.9 %fusion.22 = f32[32,32,512]{2,0,1:T(8,128)} fusion(f32[1,32,32,512]{3,2,0,1:T(8,128)} %all-to-all-done.4), kind=kOutput, calls=%fused_computation.28 | convolution fusion | flops 201349120 | bytes 4194304 | tf_op jit(solution)/shard_map/jk,kabc->jabc/dot_general | solution.py:48
  283.4 45.5 %all-to-all-done.3 = f32[1,32,32,512]{3,2,0,1:T(8,128)S(1)} async-done(((f32[1,32,32,512]{3,2,0,1:T(8,128)}), f32[1,32,32,512]{3,2,0,1:T(8,128)S(1)}, u32[]{:S(2)}, u32[]{:S(2)}) %all-to-all-start.3) | async-done | bytes 2097184 | tf_op jit(solution)/shard_map/all_to_all | solution.py:133
  328.9 4.7 fusion.49
  336.2 4.9 all-to-all-start.5
  348.5 4.8 fusion.11
  353.3 39.5 %all-to-all-done.5 = f32[32,1,32,512]{3,2,1,0:T(8,128)} async-done(((f32[32,1,32,512]{3,2,1,0:T(8,128)}), f32[32,1,32,512]{3,2,1,0:T(8,128)}, u32[]{:S(2)}, u32[]{:S(2)}) %all-to-all-start.5) | async-done | bytes 2097184 | tf_op jit(solution)/shard_map/all_to_all | solution.py:135
  392.8 8.0 %fusion.9 = f32[1,32,32,512]{3,1,2,0:T(8,128)S(1)} fusion(f32[1,32,32,512]{3,1,2,0:T(8,128)S(1)} %copy-done.2, f32[32,512,32]{1,2,0:T(8,128)} %fusion.11, f32[32,1,32,512]{3,2,1,0:T(8,128)} %all-to-all-done.5, f32[32,512,32]{1,2,0:T(8,128)} %fusion.70, f32[32,32]{0,1:T(8,128)S(1)} %copy.50, f32[32,512]{1,0:T(8,128)S(1)} %get-tuple-element.42), kind=kOutput, calls=%fused_computation.12 | convolution fusion | flops 205543424 | bytes 10555392 | tf_op jit(solution)/shard_map/jk,akbc->ajbc/dot_general | solution.py:48
  402.2 14.1 %fusion.50 = f32[512,4]{1,0:T(8,128)} fusion(f32[4,32,32]{1,0,2:T(4,128)S(1)} %copy.67, f32[1,32,32,512]{3,1,2,0:T(8,128)S(1)} %fusion.9), kind=kOutput, calls=%fused_computation.55 | convolution fusion | flops 25165824 | bytes 2121728 | tf_op jit(solution)/shard_map/dot_general | solution.py:143
  416.4 4.1 copy.66
  420.5 75.5 %reduce-scatter.4.cloned.1.call-done = f32[16,4]{1,0:T(8,128)} async-done(((f32[512,4]{1,0:T(8,128)}), f32[16,4]{1,0:T(8,128)}) %reduce-scatter.4.cloned.1.call-update) | async-done | bytes 272
  (66 shorter events, 37.1 us)
Async XLA Ops:
  7.2 13.0 %copy-start.5 = (f32[2,2,256]{2,1,0:T(2,128)S(1)}, f32[2,2,256]{2,1,0:T(2,128)}, u32[]{:S(2)}) copy-start(f32[2,2,256]{2,1,0:T(2,128)} %param.4) | copy-start | bytes 12292
  7.2 59.9 %copy-start = (f32[1,32,32,512]{3,2,1,0:T(8,128)S(1)}, f32[1,32,32,512]{3,2,1,0:T(8,128)}, u32[]{:S(2)}) copy-start(f32[1,32,32,512]{3,2,1,0:T(8,128)} %param.3) | copy-start | bytes 6291460
  7.2 63.7 %all-to-all-start.1 = ((f32[1,32,32,512]{3,2,0,1:T(8,128)}), f32[1,32,32,512]{3,2,0,1:T(8,128)}, u32[]{:S(2)}, u32[]{:S(2)}) async-start(f32[1,32,32,512]{3,2,0,1:T(8,128)} %bitcast.172), calls=%async_computation.1 | async-start | bytes 4194304 | tf_op jit(solution)/shard_map/all_to_all | solution.py:132
  20.2 41.0 %collective-permute-start = (f32[2,1,256]{2,1,0:T(1,128)S(1)}, f32[2,1,256]{2,1,0:T(1,128)S(1)}, u32[]{:S(2)}, u32[]{:S(2)}) collective-permute-start(f32[2,1,256]{2,1,0:T(1,128)S(1)} %get-tuple-element.32), channel_id=1, source_target_pairs={{32,0},{64,32},{96,64},{128,96},{160,128},{192,160},{224,192},{0,2... | collective-permute-start | bytes 6152 | tf_op jit(solution)/shard_map/ppermute | solution.py:26
  23.2 43.8 %collective-permute-start.1 = (f32[2,1,256]{2,1,0:T(1,128)S(1)}, f32[2,1,256]{2,1,0:T(1,128)S(1)}, u32[]{:S(2)}, u32[]{:S(2)}) collective-permute-start(f32[2,1,256]{2,1,0:T(1,128)S(1)} %get-tuple-element.33), channel_id=1, source_target_pairs={{0,32},{32,64},{64,96},{96,128},{128,160},{160,192},{192,224},{224... | collective-permute-start | bytes 6152 | tf_op jit(solution)/shard_map/ppermute | solution.py:25
  70.9 62.5 %all-to-all-start = ((f32[1,32,32,512]{3,2,0,1:T(8,128)}), f32[1,32,32,512]{3,2,0,1:T(8,128)}, u32[]{:S(2)}, u32[]{:S(2)}) async-start(f32[1,32,32,512]{3,2,0,1:T(8,128)} %copy.44), calls=%async_computation | async-start | bytes 4194304 | tf_op jit(solution)/shard_map/all_to_all | solution.py:133
  141.3 58.5 %all-to-all-start.2 = ((f32[32,1,32,512]{3,2,1,0:T(8,128)}), f32[32,1,32,512]{3,2,1,0:T(8,128)}, u32[]{:S(2)}, u32[]{:S(2)}) async-start(f32[32,1,32,512]{3,2,1,0:T(8,128)} %copy.48), calls=%async_computation.2 | async-start | bytes 4194304 | tf_op jit(solution)/shard_map/all_to_all | solution.py:135
  211.6 1.3 copy-start.1
  215.5 5.7 %copy-start.4 = (f32[1,32,32,512]{3,1,2,0:T(8,128)S(1)}, f32[1,32,32,512]{3,1,2,0:T(8,128)}, u32[]{:S(2)}) copy-start(f32[1,32,32,512]{3,1,2,0:T(8,128)} %get-tuple-element.44) | copy-start | bytes 6291460
  215.5 57.2 %all-to-all-start.4 = ((f32[1,32,32,512]{3,2,0,1:T(8,128)}), f32[1,32,32,512]{3,2,0,1:T(8,128)}, u32[]{:S(2)}, u32[]{:S(2)}) async-start(f32[1,32,32,512]{3,2,0,1:T(8,128)} %copy.57), calls=%async_computation.4 | async-start | bytes 4194304 | tf_op jit(solution)/shard_map/all_to_all | solution.py:132
  272.7 56.2 %all-to-all-start.3 = ((f32[1,32,32,512]{3,2,0,1:T(8,128)}), f32[1,32,32,512]{3,2,0,1:T(8,128)S(1)}, u32[]{:S(2)}, u32[]{:S(2)}) async-start(f32[1,32,32,512]{3,2,0,1:T(8,128)} %copy.55), calls=%async_computation.3 | async-start | bytes 4194304 | tf_op jit(solution)/shard_map/all_to_all | solution.py:133
  336.2 5.5 %copy-start.6 = (f32[3,16]{1,0:T(4,128)S(1)}, f32[3,16]{1,0:T(4,128)}, u32[]{:S(2)}) copy-start(f32[3,16]{1,0:T(4,128)} %param.5) | copy-start | bytes 580
  336.2 5.5 %copy-start.2 = (f32[1,32,32,512]{3,1,2,0:T(8,128)S(1)}, f32[1,32,32,512]{3,1,2,0:T(8,128)}, u32[]{:S(2)}) copy-start(f32[1,32,32,512]{3,1,2,0:T(8,128)} %copy-done.1) | copy-start | bytes 6291460
  336.2 56.6 %all-to-all-start.5 = ((f32[32,1,32,512]{3,2,1,0:T(8,128)}), f32[32,1,32,512]{3,2,1,0:T(8,128)}, u32[]{:S(2)}, u32[]{:S(2)}) async-start(f32[32,1,32,512]{3,2,1,0:T(8,128)} %copy.59), calls=%async_computation.5 | async-start | bytes 4194304 | tf_op jit(solution)/shard_map/all_to_all | solution.py:135
  341.1 154.9 %reduce-scatter.4.cloned.1.call-start = ((), (), s32[]{:S(2)}) async-start(), calls=%async_computation.7 | async-start | bytes 270336
  400.9 1.4 copy-start.3
Sparse Core Ops, SparseCore 0:
  416.5 79.4 reduce-scatter.3
where the time goes:
time: 511 us; the launch traced here: 505 us
  waiting for transfers between devices  335 us (66%)
  matrix products  77.5 us (15%)
  starting transfers between devices  50.8 us (10%)
  local copies, waits for them, and re-layouts  21.9 us (4%)
  between operations  16.5 us (3%)
    all_to_all x2, waiting for transfers between devices, on_device(): lax.all_to_all(drift_a * current, 'conf', split_axis=1, concat_axis=0, ti...  89.5 us
    all_to_all x2, waiting for transfers between devices, on_device(): lax.all_to_all(derive(along_flux_term, 0, diff_matrix), 'conf', split_axi...  81.2 us
    unnamed x2, waiting for transfers between devices  75.5 us
    dot_general x12, matrix products, derive(): jnp.einsum(patterns[which_axis], diff_matrix, values, precision=lax.Preci...  63.4 us
    all_to_all x2, waiting for transfers between devices, on_device(): lax.all_to_all(current, 'conf', split_axis=1, concat_axis=0, tiled=True)  48.9 us
    ppermute x1, waiting for transfers between devices, extended(): after = lax.ppermute(initial, axis, down)  33.7 us
    all_to_all x2, starting transfers between devices, on_device(): lax.all_to_all(current, 'conf', split_axis=1, concat_axis=0, tiled=True)  18.7 us
    all_to_all x2, starting transfers between devices, on_device(): lax.all_to_all(drift_a * current, 'conf', split_axis=1, concat_axis=0, ti...  17.3 us
  transfers between devices with their start and end apart: 9, of which 8 were waited for; matrix products, arithmetic and copies ran while one was open for 9% of the time, Pallas kernels for 0%

commit v1 on v0

v1 whole, which is shorter than its diff:
```python
import functools

import jax
import jax.numpy as jnp
import ml_dtypes
import numpy as np
from jax import lax
from jax.experimental import pallas as pl
from jax.experimental.pallas import tpu as pltpu
from jax.sharding import PartitionSpec as P

STEPS = 2
half_extent = 3.0
fene_limit = 50.0
diffusion = 0.5
time_step = 0.001
polymer_eta = 1.0
solvent_eta = 0.5
short_relax = 0.01

MESH = pl.DeviceIdType.MESH
Q = 32
GROUP = 32
OWN = 16
PART = 8
PARTS = 2
LANES = Q * PART
CELLS = GROUP * OWN


def operators():
    offsets = np.arange(Q)[:, None] - np.arange(Q)[None, :]
    angle = offsets * (np.pi / Q)
    sine = np.where(offsets == 0, 1.0, np.sin(angle))
    first = np.where(offsets % 2 == 0, 1.0, -1.0) * np.cos(angle) / sine * (np.pi / (2 * half_extent))
    first = np.where(offsets == 0, 0.0, first)
    pair = (-time_step * first, time_step * diffusion * (first @ first))
    eye = np.eye(8)

    def parts(matrix):
        high = matrix.astype(np.float32).astype(ml_dtypes.bfloat16)
        low = (matrix - high.astype(np.float64)).astype(np.float32).astype(ml_dtypes.bfloat16)
        return [high, high, low]

    along_a = np.concatenate([q for m in pair for q in parts(np.kron(m, eye))], axis=1)
    along_b = np.concatenate([q for m in pair for q in parts(np.kron(eye, m))], axis=1)
    along_c = np.concatenate([q for m in pair for q in parts(np.kron(m.T, eye))], axis=0)
    return along_a, along_b, along_c


def springs():
    coords = -half_extent + (np.arange(Q) + 0.5) * (2 * half_extent / Q)
    squares = coords * coords
    total = squares[:, None, None] + squares[None, :, None] + squares[None, None, :]
    spring = 1.0 / (1.0 - total / fene_limit)
    return np.repeat(spring, PART, axis=2).astype(np.float32)


def coord(index):
    return -half_extent + (index.astype(jnp.float32) + 0.5) * (2.0 * half_extent / Q)


def split(value):
    high = value.astype(jnp.bfloat16)
    low = (value - high.astype(jnp.float32)).astype(jnp.bfloat16)
    return [high, low, high]


def exchange_lanes(values):
    lane = lax.broadcasted_iota(jnp.int32, (8, 128), 1)
    values = list(values)
    for bit in (1, 2, 4, 8):
        upper = (lane & (8 * bit)) != 0
        shift = 8 * bit
        for i in range(16):
            if i & bit:
                continue
            one, two = values[i], values[i | bit]
            values[i] = jnp.where(upper, pltpu.roll(two, shift, 1), one)
            values[i | bit] = jnp.where(upper, two, pltpu.roll(one, 128 - shift, 1))
    return values


def exact_dot(one, two):
    return jnp.dot(one, two, precision=lax.Precision.HIGHEST, preferred_element_type=jnp.float32)


def relax(stress, gradient):
    stress_xx, stress_xy, stress_yy = stress
    for _ in range(STEPS):
        next_xx = stress_xx + time_step * (
            2.0 * (gradient[0] * stress_xx + gradient[1] * stress_xy)
            - (stress_xx - 2.0 * solvent_eta * gradient[0]) / short_relax
        )
        next_xy = stress_xy + time_step * (
            gradient[0] * stress_xy
            + gradient[1] * stress_yy
            + gradient[2] * stress_xx
            + gradient[3] * stress_xy
            - (stress_xy - solvent_eta * (gradient[1] + gradient[2])) / short_relax
        )
        next_yy = stress_yy + time_step * (
            2.0 * (gradient[2] * stress_xy + gradient[3] * stress_yy)
            - (stress_yy - 2.0 * solvent_eta * gradient[3]) / short_relax
        )
        stress_xx, stress_xy, stress_yy = next_xx, next_xy, next_yy
    return stress_xx, stress_xy, stress_yy


def kernel(
    density_hbm, velocity, short, wa_hbm, wb_hbm, wc_hbm, spring_hbm,
    out_hbm, short_out, total_out,
    density, out, packed, grid, back, change, spring, wa, wb, wc, halo, lanes, sums, moments,
    in_send, in_recv, out_send, out_recv, load_sem, halo_send, halo_recv, read_sem, write_sem,
):
    me = lax.axis_index("conf")
    my_y, my_z, my_c = me // 8, (me // 2) % 4, me % 2
    brick = lax.axis_index("cell")
    bricks = lax.axis_size("cell")
    above, below = lax.rem(brick + bricks - 1, bricks), lax.rem(brick + 1, bricks)

    reads = [
        pltpu.make_async_copy(density_hbm.at[:, pl.ds(i * 128, 128)], density.at[i], read_sem.at[i])
        for i in range(4)
    ]
    for read in reads:
        read.start()
    barrier = pltpu.get_barrier_semaphore()

    def greet(turn, carry):
        pl.semaphore_signal(barrier, inc=1, device_id={"conf": lax.rem(me + turn, GROUP)}, device_id_type=MESH)
        return carry

    lax.fori_loop(1, GROUP, greet, 0)
    for other in (above, below):
        pl.semaphore_signal(barrier, inc=1, device_id={"cell": other}, device_id_type=MESH)

    loads = [
        pltpu.make_async_copy(source, target, load_sem.at[i])
        for i, (source, target) in enumerate(((wa_hbm, wa), (wb_hbm, wb), (wc_hbm, wc), (spring_hbm, spring)))
    ]
    for load in loads:
        load.start()

    def peer(dy, turn):
        dz, dc = turn // 2, turn % 2
        return lax.rem(my_y + dy, 4) * 8 + lax.rem(my_z + dz, 4) * 2 + lax.rem(my_c + dc, 2)

    def pack(block):
        def piece(turn, carry):
            tile, half = turn // 2, turn % 2
            values = [
                density[block, pl.ds(tile * 256 + half * 16 + i, 8, stride=Q), :] for i in range(16)
            ]
            values = exchange_lanes(values)
            for i in range(16):
                packed[
                    i % 2, block * 8 + i // 2, pl.ds(pl.multiple_of(tile * 8, 8), 8),
                    pl.ds(pl.multiple_of(half * 128, 128), 128),
                ] = values[i]
            return carry

        lax.fori_loop(0, 8, piece, 0)

    def send_in(part, dy):
        def one(turn, carry):
            target = peer(dy, turn)
            pltpu.make_async_remote_copy(
                packed.at[part, target], grid.at[part, me], in_send.at[part], in_recv.at[part],
                device_id={"conf": target}, device_id_type=MESH,
            ).start()
            return carry

        lax.fori_loop(jnp.where(dy == 0, 1, 0), 8, one, 0)

    for read in reads:
        read.wait()
    pack(my_y)
    pl.semaphore_wait(barrier, GROUP + 1)
    to_above = pltpu.make_async_remote_copy(
        velocity, halo.at[1], halo_send.at[0], halo_recv.at[1], device_id={"cell": above}, device_id_type=MESH
    )
    to_below = pltpu.make_async_remote_copy(
        velocity, halo.at[0], halo_send.at[1], halo_recv.at[0], device_id={"cell": below}, device_id_type=MESH
    )
    to_above.start()
    to_below.start()
    send_in(0, jnp.int32(0))

    def pack_and_send(dy, carry):
        pack(lax.rem(my_y + dy, 4))
        send_in(0, dy)
        return carry

    lax.fori_loop(1, 4, pack_and_send, 0)

    def send_late(dy, carry):
        send_in(1, dy)
        return carry

    lax.fori_loop(0, 4, send_late, 0)
    for part in range(PARTS):
        pltpu.make_async_copy(packed.at[part, me], grid.at[part, me], in_recv.at[part]).start()

    to_above.wait()
    to_below.wait()
    rows = velocity.shape[1]
    first_row = me < GROUP // 2
    picked = []
    for i in range(2):
        here = velocity[i]
        along = (pltpu.roll(here, here.shape[1] - 1, 1) - pltpu.roll(here, 1, 1)) * 0.5
        before, after = halo[0, i], halo[1, i]
        picked.append(jnp.where(first_row, along[0:1], along[1:2]))
        down_first = (here[1:2] - before[rows - 1 : rows]) * 0.5
        down_last = (after[0:1] - here[rows - 2 : rows - 1]) * 0.5
        picked.append(jnp.where(first_row, down_first, down_last))
    picked = jnp.concatenate(picked + [jnp.zeros((4, picked[0].shape[1]), jnp.float32)], axis=0)
    width = picked.shape[1]
    offset = lax.rem(me, GROUP // 2) * OWN
    source = lax.broadcasted_iota(jnp.int32, (width, LANES), 0) - offset
    lane = lax.broadcasted_iota(jnp.int32, (width, LANES), 1)
    for part in range(PARTS):
        choose = (source == (lane & (PART - 1)) + part * PART).astype(jnp.float32)
        lanes[part] = exact_dot(picked, choose)
    own_source = lax.broadcasted_iota(jnp.int32, (width, 128), 0) - offset
    own_lane = lax.broadcasted_iota(jnp.int32, (width, 128), 1)
    own = exact_dot(picked, ((own_source == own_lane) & (own_lane < OWN)).astype(jnp.float32))
    relaxed = relax(
        tuple(short[i : i + 1, :] for i in range(3)), tuple(own[i : i + 1, :OWN] for i in range(4))
    )
    for i in range(3):
        short_out[i : i + 1, :] = relaxed[i]
    moments[...] = jnp.zeros_like(moments)
    for load in loads:
        load.wait()

    coord_c = coord(lax.broadcasted_iota(jnp.int32, (1, 1, LANES), 2) // PART)
    coord_all = coord(lax.broadcasted_iota(jnp.int32, (1, Q, 1), 1))

    def advance(part, last):
        k11, k12, k21, k22 = (lanes[part, i : i + 1, :].reshape(1, 1, LANES) for i in range(4))

        def first_direction(tile, carry):
            window = pl.ds(pl.multiple_of(tile * 8, 8), 8)
            value = grid[part, :, window, :]
            coord_a = coord(lax.broadcasted_iota(jnp.int32, (Q, 1, 1), 0))
            coord_b = coord(lax.broadcasted_iota(jnp.int32, (1, 8, 1), 1) + tile * 8)
            drift = (k11 - diffusion * spring[:, window, :]) * coord_a + k12 * coord_b
            moved = (drift * value).reshape(Q * 8, LANES)
            terms = jnp.concatenate(split(moved) + split(value.reshape(Q * 8, LANES)), axis=0)
            result = jnp.dot(wa[...], terms, preferred_element_type=jnp.float32)
            change[:, window, :] = result.reshape(Q, 8, LANES)
            return carry

        lax.fori_loop(0, 4, first_direction, 0)

        def other_directions(tile, carry):
            window = pl.ds(tile * 8, 8)
            value = grid[part, window]
            stiff = spring[window]
            coord_a = coord(lax.broadcasted_iota(jnp.int32, (8, 1, 1), 0) + tile * 8)
            pull = diffusion * stiff
            drift_b = k21 * coord_a + (k22 - pull) * coord_all
            moved_b = (drift_b * value).reshape(8 * Q, LANES)
            moved_c = (-pull * coord_c * value).reshape(8 * Q, LANES)
            plain = split(value.reshape(8 * Q, LANES))
            terms_b = jnp.concatenate(split(moved_b) + plain, axis=0)
            part_b = jnp.dot(wb[...], terms_b, preferred_element_type=jnp.float32)
            terms_c = jnp.concatenate(split(moved_c) + plain, axis=1)
            part_c = jnp.dot(terms_c, wc[...], preferred_element_type=jnp.float32)
            value = value + (change[window] + (part_b + part_c).reshape(8, Q, LANES))
            grid[part, window] = value
            if last:
                weighted = stiff * value
                sums[0] += jnp.sum(weighted, axis=0)
                weighted = weighted * coord_a
                sums[1] += jnp.sum(weighted, axis=0)
                sums[2] += jnp.sum(weighted * coord_a, axis=0)
                sums[3] += jnp.sum(value, axis=0)
            return carry

        lax.fori_loop(0, 4, other_directions, 0)

    def whole(part, carry):
        pltpu.make_async_copy(grid.at[part], grid.at[part], in_recv.at[part]).wait()
        sums[...] = jnp.zeros_like(sums)
        for turn in range(STEPS):
            advance(part, turn == STEPS - 1)

        def send_out(turn, inner):
            target = peer(turn // 8, lax.rem(turn, 8))
            pltpu.make_async_remote_copy(
                grid.at[part, target], back.at[part, me], out_send.at[part], out_recv.at[part],
                device_id={"conf": target}, device_id_type=MESH,
            ).start()
            return inner

        lax.fori_loop(1, GROUP, send_out, 0)
        pltpu.make_async_copy(grid.at[part, me], back.at[part, me], out_recv.at[part]).start()
        column = coord(lax.broadcasted_iota(jnp.int32, (Q, 1), 0))
        scale = 1.0 / float(Q**3)
        stacked = jnp.concatenate(
            [
                jnp.sum(sums[2], axis=0, keepdims=True),
                jnp.sum(sums[1] * column, axis=0, keepdims=True),
                jnp.sum(sums[0] * (column * column), axis=0, keepdims=True),
                jnp.sum(sums[3], axis=0, keepdims=True),
                jnp.zeros((4, LANES), jnp.float32),
            ],
            axis=0,
        )
        fold_row = lax.broadcasted_iota(jnp.int32, (LANES, 128), 0) & (PART - 1)
        fold_lane = lax.broadcasted_iota(jnp.int32, (LANES, 128), 1) - part * PART
        moments[...] += exact_dot(stacked * scale, (fold_row == fold_lane).astype(jnp.float32))
        return carry

    lax.fori_loop(0, PARTS, whole, 0)

    total = moments[...]
    for i, polymer in enumerate(
        (
            polymer_eta * (total[0:1] - total[3:4]),
            polymer_eta * total[1:2],
            polymer_eta * (total[2:3] - total[3:4]),
        )
    ):
        total_out[i : i + 1, :] = polymer[:, :OWN] + short_out[i : i + 1, :]

    for part in range(PARTS):
        pltpu.make_async_copy(back.at[part], back.at[part], out_recv.at[part]).wait()

    def unpack(block, carry):
        def piece(turn, inner):
            tile, half = turn // 2, turn % 2
            values = [
                back[
                    i % 2, block * 8 + i // 2, pl.ds(pl.multiple_of(tile * 8, 8), 8),
                    pl.ds(pl.multiple_of(half * 128, 128), 128),
                ]
                for i in range(16)
            ]
            values = exchange_lanes(values)
            for i in range(16):
                out[block, pl.ds(tile * 256 + half * 16 + i, 8, stride=Q), :] = values[i]
            return inner

        lax.fori_loop(0, 8, piece, 0)
        pltpu.make_async_copy(
            out.at[block], out_hbm.at[:, pl.ds(pl.multiple_of(block * 128, 128), 128)], write_sem.at[block]
        ).start()
        return carry

    lax.fori_loop(0, 4, unpack, 0)
    for i in range(4):
        pltpu.make_async_copy(out.at[i], out_hbm.at[:, pl.ds(i * 128, 128)], write_sem.at[i]).wait()
    others = pl.ds(0, GROUP - 1)
    for part in range(PARTS):
        pltpu.make_async_copy(packed.at[part, others], packed.at[part, others], in_send.at[part]).wait()
        pltpu.make_async_copy(grid.at[part, others], grid.at[part, others], out_send.at[part]).wait()


def on_device(density, velocity, short_stress):
    along_a, along_b, along_c = operators()
    spring = springs()
    vmem = pl.BlockSpec(memory_space=pltpu.VMEM)
    anywhere = pl.BlockSpec(memory_space=pl.ANY)
    blocks = (PARTS, GROUP, Q, LANES)
    dma = pltpu.SemaphoreType.DMA
    result, short_next, total_stress = pl.pallas_call(
        kernel,
        name="fokker_planck",
        out_shape=(
            jax.ShapeDtypeStruct((Q * Q, CELLS), jnp.float32),
            jax.ShapeDtypeStruct((3, OWN), jnp.float32),
            jax.ShapeDtypeStruct((3, OWN), jnp.float32),
        ),
        in_specs=[anywhere, vmem, vmem, anywhere, anywhere, anywhere, anywhere],
        out_specs=(anywhere, vmem, vmem),
        scratch_shapes=[
            pltpu.VMEM((4, Q * Q, 128), jnp.float32),
            pltpu.VMEM((4, Q * Q, 128), jnp.float32),
            pltpu.VMEM(blocks, jnp.float32),
            pltpu.VMEM(blocks, jnp.float32),
            pltpu.VMEM(blocks, jnp.float32),
            pltpu.VMEM((Q, Q, LANES), jnp.float32),
            pltpu.VMEM(spring.shape, jnp.float32),
            pltpu.VMEM(along_a.shape, jnp.bfloat16),
            pltpu.VMEM(along_b.shape, jnp.bfloat16),
            pltpu.VMEM(along_c.shape, jnp.bfloat16),
            pltpu.VMEM((2,) + velocity.shape, jnp.float32),
            pltpu.VMEM((PARTS, 8, LANES), jnp.float32),
            pltpu.VMEM((4, Q, LANES), jnp.float32),
            pltpu.VMEM((8, 128), jnp.float32),
            dma((PARTS,)),
            dma((PARTS,)),
            dma((PARTS,)),
            dma((PARTS,)),
            dma((4,)),
            dma((2,)),
            dma((2,)),
            dma((4,)),
            dma((4,)),
        ],
        compiler_params=pltpu.CompilerParams(
            collective_id=0, has_side_effects=True, vmem_limit_bytes=48 * 1024 * 1024
        ),
    )(
        density.reshape(Q * Q, CELLS),
        velocity,
        short_stress,
        along_a,
        along_b,
        along_c,
        spring,
    )
    return result.reshape(density.shape), short_next, total_stress


def solution(mesh):
    return jax.shard_map(
        on_device,
        mesh=mesh,
        in_specs=(P("conf", None, None, "cell"), P(None, "cell", None), P(None, ("cell", "conf"))),
        out_specs=(
            P("conf", None, None, "cell"),
            P(None, ("cell", "conf")),
            P(None, ("cell", "conf")),
        ),
        check_vma=False,
    )
```

time: 511 us -> 124 us (0.24); the launches traced: 505 us -> 124 us
  waiting for transfers between devices: 335 us -> 0 us
  Pallas kernels: 0 us -> 115 us
  matrix products: 77.5 us -> 0 us
  starting transfers between devices: 50.8 us -> 0 us
  between operations: 16.5 us -> 0.65 us
  local copies, waits for them, and re-layouts: 21.9 us -> 8.46 us
    all_to_all x6 -> x0, waiting for transfers between devices: 220 us -> none  [the longest x2 89.5 us: on_device(): lax.all_to_all(drift_a * current, 'conf', split_axis=1, concat_axis=0, ti...]
    pallas_call x0 -> x1, Pallas kernels: none -> 115 us  [on_device(): pl.pallas_call(kernel, name='fokker_planck', out_shape=(jax.ShapeDtypeStr...]
    dot_general x13 -> x0, matrix products: 77.5 us -> none  [the longest x12 63.4 us: derive(): jnp.einsum(patterns[which_axis], diff_matrix, values, precision=lax.Preci...]
    unnamed x2 -> x0, waiting for transfers between devices: 75.5 us -> none
    all_to_all x6 -> x0, starting transfers between devices: 47.6 us -> none  [the longest x2 18.7 us: on_device(): lax.all_to_all(current, 'conf', split_axis=1, concat_axis=0, tiled=True)]
    ppermute x2 -> x0, waiting for transfers between devices: 39.5 us -> none  [the longest x1 33.7 us: extended(): after = lax.ppermute(initial, axis, down)]
    mul x5 -> x0, local copies, waits for them, and re-layouts: 5.32 us -> none  [the longest x2 5.09 us: on_device(): drift_a * current]
  transfers between devices with their start and end apart: 9 -> 0, of which waited for: 8 -> 0; matrix products, arithmetic and copies ran while one was open for 9% -> 0% of each run, Pallas kernels for 0% -> 0%
where the time goes in v1:
time: 124 us
  Pallas kernels  115 us (93%)
  local copies, waits for them, and re-layouts  8.46 us (7%)
    pallas_call x1, Pallas kernels, on_device(): pl.pallas_call(kernel, name='fokker_planck', out_shape=(jax.ShapeDtypeStr...  115 us
    unnamed x15, local copies, waits for them, and re-layouts  8.46 us

profile of v1, /device:TPU:1, one launch (start us, length us, event | category | flops | bytes accessed | tf_op | source)
XLA Modules:
  0.0 124.0 jit_solution(7742363681363041837)
XLA Ops:
  0.6 0.0 copy-start
  0.6 1.2 copy-done
  1.9 0.0 copy-start.1
  1.9 1.1 copy-done.1
  3.0 0.0 copy-start.2
  3.0 1.1 copy-done.2
  4.1 0.0 copy-start.3
  4.1 1.1 copy-done.3
  5.3 0.0 copy-start.4
  5.3 0.7 copy-done.4
  5.9 0.0 copy-start.5
  5.9 0.7 copy-done.5
  6.6 114.9 %fokker_planck.1 = (f32[1024,512]{1,0:T(8,128)S(1)}, f32[3,16]{1,0:T(4,128)S(1)}, f32[3,16]{1,0:T(4,128)S(1)}) custom-call(f32[1024,512]{1,0:T(8,128)} %bitcast.3, f32[2,2,256]{2,1,0:T(2,128)S(1)} %copy-done.4, f32[3,16]{1,0:T(4,128)S(1)} %copy-done.5, bf16[256,1536]{1,0:T(8,128)(2,1)S(1)} %copy-done.3, bf16[256,1536]{1,0:T(8,128)(2,1)S(1)} %copy-done.2, ...), custom_call_target="tpu_custom_call" | custom-call | tf_op jit(solution)/shard_map/fokker_planck/pallas_call | solution.py:370
  121.5 1.3 %copy.13 = f32[1,32,32,512]{3,2,1,0:T(8,128)} copy(f32[1,32,32,512]{3,2,1,0:T(8,128)S(1)} %bitcast.2) | data formatting | bytes 4194304
  122.9 0.6 copy.14
  123.4 0.6 copy.15
Async XLA Ops:
  0.6 1.2 copy-start
  1.9 1.1 copy-start.1
  3.0 1.1 copy-start.2
  4.1 1.1 copy-start.3
  5.3 0.7 copy-start.4
  5.9 0.7 copy-start.5

commit v2 on v1

v2 whole, which is shorter than its diff:
```python
import functools

import jax
import jax.numpy as jnp
import numpy as np
from jax import lax
from jax.experimental import pallas as pl
from jax.experimental.pallas import tpu as pltpu
from jax.sharding import PartitionSpec as P

STEPS = 2
half_extent = 3.0
fene_limit = 50.0
diffusion = 0.5
time_step = 0.001
polymer_eta = 1.0
solvent_eta = 0.5
short_relax = 0.01

MESH = pl.DeviceIdType.MESH
Q = 32
GROUP = 32
OWN = 16
PART = 8
PARTS = 2
LANES = Q * PART
CELLS = GROUP * OWN
TALL = 32
VMEM_LIMIT = 61 * 1024 * 1024


def stencils():
    offsets = np.arange(Q)[:, None] - np.arange(Q)[None, :]
    angle = offsets * (np.pi / Q)
    sine = np.where(offsets == 0, 1.0, np.sin(angle))
    first = np.where(offsets % 2 == 0, 1.0, -1.0) * np.cos(angle) / sine * (np.pi / (2 * half_extent))
    first = np.where(offsets == 0, 0.0, first)
    return (-time_step * first)[:, 0], (time_step * diffusion * (first @ first))[:, 0]


def build_operators(wa, wb, wc):
    first, second = stencils()
    size = 8 * Q
    row = lax.broadcasted_iota(jnp.int32, (size, size), 0)
    column = lax.broadcasted_iota(jnp.int32, (size, size), 1)

    def circulant(offset, inside):
        key = jnp.where(inside, offset & (Q - 1), -1)
        one, two = (jnp.zeros((size, size), jnp.float32) for _ in range(2))
        for i in range(Q):
            here = key == i
            one = jnp.where(here, jnp.float32(first[i]), one)
            two = jnp.where(here, jnp.float32(second[i]), two)
        return one, two

    def store(ref, matrix, at, by_row):
        high, low, again = split(matrix)
        for i, value in enumerate((high, again, low)):
            place = pl.ds((at + i) * size, size)
            if by_row:
                ref[place, :] = value
            else:
                ref[:, place] = value

    one, two = circulant((row >> 3) - (column >> 3), (row & 7) == (column & 7))
    store(wa, one, 0, False)
    store(wa, two, 3, False)
    store(wc, -one, 0, True)
    store(wc, two, 3, True)
    one, two = circulant(row - column, (row >> 5) == (column >> 5))
    store(wb, one, 0, False)
    store(wb, two, 3, False)


def coord(index):
    return -half_extent + (index.astype(jnp.float32) + 0.5) * (2.0 * half_extent / Q)


def split(value):
    high = value.astype(jnp.bfloat16)
    low = (value - high.astype(jnp.float32)).astype(jnp.bfloat16)
    return [high, low, high]


def exchange_lanes(values):
    lane = lax.broadcasted_iota(jnp.int32, values[0].shape, 1)
    values = list(values)
    for bit in (1, 2, 4, 8):
        upper = (lane & (8 * bit)) != 0
        shift = 8 * bit
        for i in range(16):
            if i & bit:
                continue
            one, two = values[i], values[i | bit]
            mixed = jnp.where(upper, one, two)
            if shift == 64:
                mixed = pltpu.roll(mixed, 64, 1)
            else:
                mixed = jnp.take_along_axis(mixed, lane ^ shift, axis=1, mode="promise_in_bounds")
            values[i] = jnp.where(upper, mixed, one)
            values[i | bit] = jnp.where(upper, two, mixed)
    return values


def unpack(arrived, target, block):
    def piece(turn, carry):
        tile, half = turn // 2, turn % 2
        values = [
            arrived[
                block * 16 + i, pl.ds(pl.multiple_of(tile * TALL, TALL), TALL),
                pl.ds(pl.multiple_of(half * 128, 128), 128),
            ]
            for i in range(16)
        ]
        values = exchange_lanes(values)
        for i in range(16):
            target[pl.ds(tile * (TALL * Q) + half * 16 + i, TALL, stride=Q), :] = values[i]
        return carry

    lax.fori_loop(0, 2 * Q // TALL, piece, 0)


def exact_dot(one, two):
    return jnp.dot(one, two, precision=lax.Precision.HIGHEST, preferred_element_type=jnp.float32)


def relax(stress, gradient):
    stress_xx, stress_xy, stress_yy = stress
    for _ in range(STEPS):
        next_xx = stress_xx + time_step * (
            2.0 * (gradient[0] * stress_xx + gradient[1] * stress_xy)
            - (stress_xx - 2.0 * solvent_eta * gradient[0]) / short_relax
        )
        next_xy = stress_xy + time_step * (
            gradient[0] * stress_xy
            + gradient[1] * stress_yy
            + gradient[2] * stress_xx
            + gradient[3] * stress_xy
            - (stress_xy - solvent_eta * (gradient[1] + gradient[2])) / short_relax
        )
        next_yy = stress_yy + time_step * (
            2.0 * (gradient[2] * stress_xy + gradient[3] * stress_yy)
            - (stress_yy - 2.0 * solvent_eta * gradient[3]) / short_relax
        )
        stress_xx, stress_xy, stress_yy = next_xx, next_xy, next_yy
    return stress_xx, stress_xy, stress_yy


def kernel(
    density_hbm, velocity_hbm, short_hbm,
    early_hbm, late, stress,
    density, velocity, short, early, early_back, inbox, packed, grid, change, spring, wa, wb, wc, halo, lanes, sums, moments,
    in_send, in_recv, out_send, out_recv, load_sem, halo_send, halo_recv, read_sem,
    note_send, note_recv, write_sem,
):
    me = lax.axis_index("conf")
    my_y, my_z, my_c = me // 8, (me // 2) % 4, me % 2
    brick = lax.axis_index("cell")
    bricks = lax.axis_size("cell")
    above, below = lax.rem(brick + bricks - 1, bricks), lax.rem(brick + 1, bricks)

    reads = [
        pltpu.make_async_copy(
            density_hbm.at[:, pl.ds(pl.multiple_of(block * 128, 128), 128)], density.at[block], read_sem.at[i]
        )
        for i, block in enumerate([2 * (i // 2) + lax.rem(my_y // 2 + i, 2) for i in range(4)])
    ]
    for read in reads:
        read.start()
    barrier = pltpu.get_barrier_semaphore()

    def greet(turn, carry):
        pl.semaphore_signal(barrier, inc=1, device_id={"conf": lax.rem(me + turn, GROUP)}, device_id_type=MESH)
        return carry

    lax.fori_loop(1, GROUP, greet, 0)
    for other in (above, below):
        pl.semaphore_signal(barrier, inc=1, device_id={"cell": other}, device_id_type=MESH)

    loads = [
        pltpu.make_async_copy(source, target, load_sem.at[i])
        for i, (source, target) in enumerate(
            ((velocity_hbm, velocity), (short_hbm, short))
        )
    ]
    for load in loads:
        load.start()

    def side(turn):
        return lax.rem(my_y // 2 + turn, 2)

    def peer(half, turn):
        y = 2 * side(half) + lax.rem(my_y + turn // 8, 2)
        z = lax.rem(my_z + lax.rem(turn, 8) // 2, 4)
        return y * 8 + z * 2 + lax.rem(my_c + turn, 2)

    def pack(part, half):
        first = side(half)
        block = part * 2 + first

        def piece(turn, carry):
            tile, half = turn // 2, turn % 2
            values = [
                density[block, pl.ds(tile * (TALL * Q) + half * 16 + i, TALL, stride=Q), :] for i in range(16)
            ]
            values = exchange_lanes(values)
            for i in range(16):
                packed[
                    part, first * 16 + i, pl.ds(pl.multiple_of(tile * TALL, TALL), TALL),
                    pl.ds(pl.multiple_of(half * 128, 128), 128),
                ] = values[i]
            return carry

        lax.fori_loop(0, 2 * Q // TALL, piece, 0)

    def send_in(part, half):
        def one(turn, carry):
            target = peer(half, turn)
            pltpu.make_async_remote_copy(
                packed.at[part, target], grid.at[part, me], in_send.at[part], in_recv.at[part],
                device_id={"conf": target}, device_id_type=MESH,
            ).start()
            return carry

        lax.fori_loop(jnp.where(half == 0, 1, 0), 16, one, 0)

    reads[0].wait()
    pack(0, 0)
    pl.semaphore_wait(barrier, GROUP + 1)
    loads[0].wait()
    to_above = pltpu.make_async_remote_copy(
        velocity, halo.at[1], halo_send.at[0], halo_recv.at[1], device_id={"cell": above}, device_id_type=MESH
    )
    to_below = pltpu.make_async_remote_copy(
        velocity, halo.at[0], halo_send.at[1], halo_recv.at[0], device_id={"cell": below}, device_id_type=MESH
    )
    to_above.start()
    to_below.start()
    send_in(0, jnp.int32(0))
    for i in range(1, 4):
        reads[i].wait()
        pack(i // 2, i % 2)
        send_in(i // 2, jnp.int32(i % 2))
    for part in range(PARTS):
        pltpu.make_async_copy(packed.at[part, me], grid.at[part, me], in_recv.at[part]).start()

    to_above.wait()
    to_below.wait()
    last_row = velocity.shape[1] - 1
    gradients = [[], []]
    for i in range(2):
        here = velocity[i]
        along = (pltpu.roll(here, here.shape[1] - 1, 1) - pltpu.roll(here, 1, 1)) * 0.5
        down = (
            (here[1:2] - halo[0, i][last_row : last_row + 1]) * 0.5,
            (halo[1, i][0:1] - here[0:1]) * 0.5,
        )
        for part in range(PARTS):
            gradients[part] += [along[part : part + 1], down[part]]
    width = velocity.shape[2]
    filler = [jnp.zeros((4, width), jnp.float32)]
    gradients = [jnp.concatenate(one + filler, axis=0) for one in gradients]
    source = lax.broadcasted_iota(jnp.int32, (width, LANES), 0) - me * PART
    lane = lax.broadcasted_iota(jnp.int32, (width, LANES), 1)
    choose = (source == (lane & (PART - 1))).astype(jnp.float32)
    for part in range(PARTS):
        lanes[part] = exact_dot(gradients[part], choose)
    picked = jnp.where(me < GROUP // 2, gradients[0], gradients[1])
    offset = lax.rem(me, GROUP // 2) * OWN
    own_source = lax.broadcasted_iota(jnp.int32, (width, 128), 0) - offset
    own_lane = lax.broadcasted_iota(jnp.int32, (width, 128), 1)
    own = exact_dot(picked, ((own_source == own_lane) & (own_lane < OWN)).astype(jnp.float32))
    loads[1].wait()
    relaxed = relax(
        tuple(short[i : i + 1, :] for i in range(3)), tuple(own[i : i + 1, :OWN] for i in range(4))
    )
    for i in range(3):
        stress[i : i + 1, :OWN] = relaxed[i]
    build_operators(wa, wb, wc)

    coord_c = coord(lax.broadcasted_iota(jnp.int32, (1, 1, LANES), 2) // PART)
    coord_all = coord(lax.broadcasted_iota(jnp.int32, (1, Q, 1), 1))


    def build_springs(index, carry):
        here = coord(index)
        squares = here * here + coord_all * coord_all + coord_c * coord_c
        spring[pl.ds(index, 1)] = 1.0 / (1.0 - squares / fene_limit)
        return carry

    lax.fori_loop(0, Q, build_springs, 0)

    def advance(part, last):
        k11, k12, k21, k22 = (lanes[part, i : i + 1, :].reshape(1, 1, LANES) for i in range(4))

        def first_direction(tile, carry):
            window = pl.ds(pl.multiple_of(tile * 8, 8), 8)
            value = grid[part, :, window, :]
            coord_a = coord(lax.broadcasted_iota(jnp.int32, (Q, 1, 1), 0))
            coord_b = coord(lax.broadcasted_iota(jnp.int32, (1, 8, 1), 1) + tile * 8)
            drift = (k11 - diffusion * spring[:, window, :]) * coord_a + k12 * coord_b
            moved = (drift * value).reshape(Q * 8, LANES)
            terms = jnp.concatenate(split(moved) + split(value.reshape(Q * 8, LANES)), axis=0)
            result = jnp.dot(wa[...], terms, preferred_element_type=jnp.float32)
            change[:, window, :] = result.reshape(Q, 8, LANES)
            return carry

        lax.fori_loop(0, 4, first_direction, 0)

        def other_directions(tile, carry):
            window = pl.ds(tile * 8, 8)
            value = grid[part, window]
            stiff = spring[window]
            coord_a = coord(lax.broadcasted_iota(jnp.int32, (8, 1, 1), 0) + tile * 8)
            pull = diffusion * stiff
            drift_b = k21 * coord_a + (k22 - pull) * coord_all
            moved_b = (drift_b * value).reshape(8 * Q, LANES)
            moved_c = (-pull * coord_c * value).reshape(8 * Q, LANES)
            plain = split(value.reshape(8 * Q, LANES))
            terms_b = jnp.concatenate(split(moved_b) + plain, axis=0)
            part_b = jnp.dot(wb[...], terms_b, preferred_element_type=jnp.float32)
            terms_c = jnp.concatenate(split(moved_c) + plain, axis=1)
            part_c = jnp.dot(terms_c, wc[...], preferred_element_type=jnp.float32)
            value = value + (change[window] + (part_b + part_c).reshape(8, Q, LANES))
            grid[part, window] = value
            if last:
                weighted = stiff * value
                sums[0] += jnp.sum(weighted, axis=0)
                weighted = weighted * coord_a
                sums[1] += jnp.sum(weighted, axis=0)
                sums[2] += jnp.sum(weighted * coord_a, axis=0)
                sums[3] += jnp.sum(value, axis=0)
            return carry

        lax.fori_loop(0, 4, other_directions, 0)

    def whole(part, carry):
        pltpu.make_async_copy(grid.at[part], grid.at[part], in_recv.at[part]).wait()
        sums[...] = jnp.zeros_like(sums)
        for turn in range(STEPS):
            advance(part, turn == STEPS - 1)

        def send_to(arrived):
            def send_out(turn, inner):
                target = peer(turn // 16, lax.rem(turn, 16))
                pltpu.make_async_remote_copy(
                    grid.at[part, target], arrived.at[me], out_send.at[part], out_recv.at[part],
                    device_id={"conf": target}, device_id_type=MESH,
                ).start()
                return inner

            lax.fori_loop(1, GROUP, send_out, 0)
            pltpu.make_async_copy(grid.at[part, me], arrived.at[me], out_recv.at[part]).start()

        @pl.when(part == 0)
        def _():
            send_to(early_back)

        @pl.when(part == 1)
        def _():
            send_to(late)

        column = coord(lax.broadcasted_iota(jnp.int32, (Q, 1), 0))
        scale = 1.0 / float(Q**3)
        stacked = jnp.concatenate(
            [
                jnp.sum(sums[2], axis=0, keepdims=True),
                jnp.sum(sums[1] * column, axis=0, keepdims=True),
                jnp.sum(sums[0] * (column * column), axis=0, keepdims=True),
                jnp.sum(sums[3], axis=0, keepdims=True),
                jnp.zeros((4, LANES), jnp.float32),
            ],
            axis=0,
        )
        fold_row = lax.broadcasted_iota(jnp.int32, (LANES, 128), 0) & (PART - 1)
        fold_lane = lax.broadcasted_iota(jnp.int32, (LANES, 128), 1) - my_c * PART
        moments[part] = exact_dot(stacked * scale, (fold_row == fold_lane).astype(jnp.float32))
        owner = part * (GROUP // 2) + me // 2

        @pl.when(owner != me)
        def _():
            pltpu.make_async_remote_copy(
                moments.at[part], inbox.at[my_c], note_send.at[part], note_recv.at[my_c],
                device_id={"conf": owner}, device_id_type=MESH,
            ).start()

        @pl.when(owner == me)
        def _():
            pltpu.make_async_copy(moments.at[part], inbox.at[my_c], note_recv.at[my_c]).start()

        return carry

    lax.fori_loop(0, PARTS, whole, 0)

    for i in range(2):
        pltpu.make_async_copy(inbox.at[i], inbox.at[i], note_recv.at[i]).wait()
    total = inbox[0] + inbox[1]
    for i, polymer in enumerate(
        (
            polymer_eta * (total[0:1] - total[3:4]),
            polymer_eta * total[1:2],
            polymer_eta * (total[2:3] - total[3:4]),
        )
    ):
        stress[i + 4 : i + 5, :OWN] = polymer[:, :OWN] + stress[i : i + 1, :OWN]

    pltpu.make_async_copy(early_back, early_back, out_recv.at[0]).wait()

    def early_side(block, carry):
        unpack(early_back, early.at[block], block)
        early_write(block).start()
        return carry

    def early_write(block):
        return pltpu.make_async_copy(early.at[block], early_hbm.at[block], write_sem.at[block])

    lax.fori_loop(0, 2, early_side, 0)
    pltpu.make_async_copy(late, late, out_recv.at[1]).wait()
    for i in range(2):
        early_write(i).wait()
    others = pl.ds(0, GROUP - 1)
    for part in range(PARTS):
        pltpu.make_async_copy(packed.at[part, others], packed.at[part, others], in_send.at[part]).wait()
        pltpu.make_async_copy(grid.at[part, others], grid.at[part, others], out_send.at[part]).wait()

        @pl.when(part * (GROUP // 2) + me // 2 != me)
        def _(part=part):
            pltpu.make_async_copy(moments.at[part], moments.at[part], note_send.at[part]).wait()


def spread(early_hbm, late_hbm, stress, out_hbm, short_hbm, total_hbm, early, late, out, small, sem):
    loads = [
        pltpu.make_async_copy(late_hbm.at[pl.ds(16 * i, 16)], late.at[pl.ds(16 * i, 16)], sem.at[i]) for i in range(2)
    ]
    loads += [pltpu.make_async_copy(early_hbm.at[i], early.at[i], sem.at[2 + i]) for i in range(2)]
    for load in loads:
        load.start()
    for i in range(2):
        small[i] = stress[4 * i : 4 * i + 3, :OWN]
    copies = [
        pltpu.make_async_copy(small.at[i], target, sem.at[4 + i]) for i, target in enumerate((short_hbm, total_hbm))
    ]
    for copy in copies:
        copy.start()
    for i in range(2):
        loads[i].wait()
        unpack(late, out.at[i], i)
        loads[2 + i].wait()
        for j, source in enumerate((out, early)):
            columns = pl.ds((256 if j == 0 else 0) + i * 128, 128)
            copy = pltpu.make_async_copy(source.at[i], out_hbm.at[:, columns], sem.at[6 + 2 * i + j])
            copy.start()
            copies.append(copy)
    for copy in copies:
        copy.wait()


def on_device(density, velocity, short_stress):
    vmem = pl.BlockSpec(memory_space=pltpu.VMEM)
    hbm = pl.BlockSpec(memory_space=pltpu.HBM)
    blocks = (PARTS, GROUP, Q, LANES)
    dma = pltpu.SemaphoreType.DMA
    early, late, stress = pl.pallas_call(
        kernel,
        name="fokker_planck",
        out_shape=(
            jax.ShapeDtypeStruct((2, Q * Q, 128), jnp.float32),
            jax.ShapeDtypeStruct((GROUP, Q, LANES), jnp.float32),
            jax.ShapeDtypeStruct((8, 128), jnp.float32),
        ),
        in_specs=[hbm] * 3,
        out_specs=(hbm, vmem, vmem),
        scratch_shapes=[
            pltpu.VMEM((4, Q * Q, 128), jnp.float32),
            pltpu.VMEM(velocity.shape, jnp.float32),
            pltpu.VMEM(short_stress.shape, jnp.float32),
            pltpu.VMEM((2, Q * Q, 128), jnp.float32),
            pltpu.VMEM((GROUP, Q, LANES), jnp.float32),
            pltpu.VMEM((2, 8, 128), jnp.float32),
            pltpu.VMEM(blocks, jnp.float32),
            pltpu.VMEM(blocks, jnp.float32),
            pltpu.VMEM((Q, Q, LANES), jnp.float32),
            pltpu.VMEM((Q, Q, LANES), jnp.float32),
            pltpu.VMEM((8 * Q, 6 * 8 * Q), jnp.bfloat16),
            pltpu.VMEM((8 * Q, 6 * 8 * Q), jnp.bfloat16),
            pltpu.VMEM((6 * LANES, LANES), jnp.bfloat16),
            pltpu.VMEM((2,) + velocity.shape, jnp.float32),
            pltpu.VMEM((PARTS, 8, LANES), jnp.float32),
            pltpu.VMEM((4, Q, LANES), jnp.float32),
            pltpu.VMEM((PARTS, 8, 128), jnp.float32),
            dma((PARTS,)),
            dma((PARTS,)),
            dma((PARTS,)),
            dma((PARTS,)),
            dma((2,)),
            dma((2,)),
            dma((2,)),
            dma((4,)),
            dma((PARTS,)),
            dma((2,)),
            dma((2,)),
        ],
        compiler_params=pltpu.CompilerParams(
            collective_id=0, has_side_effects=True, vmem_limit_bytes=VMEM_LIMIT
        ),
    )(
        density.reshape(Q * Q, CELLS),
        velocity,
        short_stress,
    )
    result, short_next, total_stress = pl.pallas_call(
        spread,
        name="spread",
        out_shape=(
            jax.ShapeDtypeStruct((Q * Q, CELLS), jnp.float32),
            jax.ShapeDtypeStruct(short_stress.shape, jnp.float32),
            jax.ShapeDtypeStruct(short_stress.shape, jnp.float32),
        ),
        in_specs=[hbm, hbm, vmem],
        out_specs=(hbm, hbm, hbm),
        scratch_shapes=[
            pltpu.VMEM((2, Q * Q, 128), jnp.float32),
            pltpu.VMEM((GROUP, Q, LANES), jnp.float32),
            pltpu.VMEM((2, Q * Q, 128), jnp.float32),
            pltpu.VMEM((2,) + short_stress.shape, jnp.float32),
            dma((10,)),
        ],
        compiler_params=pltpu.CompilerParams(vmem_limit_bytes=VMEM_LIMIT),
    )(early, late, stress)
    return result.reshape(density.shape), short_next, total_stress


def solution(mesh):
    return jax.shard_map(
        on_device,
        mesh=mesh,
        in_specs=(P("conf", None, None, "cell"), P(None, "cell", None), P(None, ("cell", "conf"))),
        out_specs=(
            P("conf", None, None, "cell"),
            P(None, ("cell", "conf")),
            P(None, ("cell", "conf")),
        ),
        check_vma=False,
    )
```

time: 124 us -> 112 us (0.903)
  local copies, waits for them, and re-layouts: 8.46 us -> 0 us
  Pallas kernels: 115 us -> 111 us
    unnamed x15 -> x0, local copies, waits for them, and re-layouts: 8.46 us -> none
    pallas_call x1, Pallas kernels: 115 us -> 107 us  [on_device(): pl.pallas_call(kernel, name='fokker_planck', out_shape=(jax.ShapeDtypeStr...]
    pallas_call x0 -> x1, Pallas kernels: none -> 4.71 us  [on_device(): pl.pallas_call(spread, name='spread', out_shape=(jax.ShapeDtypeStruct((Q...]
where the time goes in v2:
time: 112 us
  Pallas kernels  111 us (99%)
    pallas_call x1, Pallas kernels, on_device(): pl.pallas_call(kernel, name='fokker_planck', out_shape=(jax.ShapeDtypeStr...  107 us
    pallas_call x1, Pallas kernels, on_device(): pl.pallas_call(spread, name='spread', out_shape=(jax.ShapeDtypeStruct((Q...  4.71 us

profile of v2, /device:TPU:1, one launch (start us, length us, event | category | flops | bytes accessed | tf_op | source)
XLA Modules:
  0.0 111.9 jit_solution(14896866072717121865)
XLA Ops:
  0.6 106.6 %fokker_planck.1 = (f32[2,1024,128]{2,1,0:T(8,128)}, f32[32,32,256]{2,1,0:T(8,128)}, f32[8,128]{1,0:T(8,128)}) custom-call(f32[1024,512]{1,0:T(8,128)} %bitcast.2, f32[2,2,256]{2,1,0:T(2,128)} %velocity_hbm.1, f32[3,16]{1,0:T(4,128)} %short_hbm.1), custom_call_target="tpu_custom_call" | custom-call | tf_op jit(solution)/shard_map/fokker_planck/pallas_call | solution.py:463
  107.2 4.7 %spread.1 = (f32[1024,512]{1,0:T(8,128)}, f32[3,16]{1,0:T(4,128)}, f32[3,16]{1,0:T(4,128)}) custom-call(f32[2,1024,128]{2,1,0:T(8,128)} %get-tuple-element.9.early_hbm, f32[32,32,256]{2,1,0:T(8,128)} %get-tuple-element.10.late_hbm, f32[8,128]{1,0:T(8,128)} %get-tuple-element.11.stress), custom_call_target="tpu_custom_call" | custom-call | tf_op jit(solution)/shard_map/spread/pallas_call | solution.py:511

commit v3 on v2

--- a/solution.py
+++ b/solution.py
@@ -26,7 +26,7 @@
 LANES = Q * PART
 CELLS = GROUP * OWN
 TALL = 32
-VMEM_LIMIT = 61 * 1024 * 1024
+VMEM_LIMIT = 50 * 1024 * 1024
 
 
 def stencils():
@@ -148,10 +148,10 @@
 
 def kernel(
     density_hbm, velocity_hbm, short_hbm,
-    early_hbm, late, stress,
-    density, velocity, short, early, early_back, inbox, packed, grid, change, spring, wa, wb, wc, halo, lanes, sums, moments,
+    early, late, stress,
+    density, velocity, short, early_back, inbox, packed, grid, change, spring, wa, wb, wc, halo, lanes, sums, moments,
     in_send, in_recv, out_send, out_recv, load_sem, halo_send, halo_recv, read_sem,
-    note_send, note_recv, write_sem,
+    note_send, note_recv,
 ):
     me = lax.axis_index("conf")
     my_y, my_z, my_c = me // 8, (me // 2) % 4, me % 2
@@ -408,16 +408,10 @@
 
     def early_side(block, carry):
         unpack(early_back, early.at[block], block)
-        early_write(block).start()
         return carry
-
-    def early_write(block):
-        return pltpu.make_async_copy(early.at[block], early_hbm.at[block], write_sem.at[block])
 
     lax.fori_loop(0, 2, early_side, 0)
     pltpu.make_async_copy(late, late, out_recv.at[1]).wait()
-    for i in range(2):
-        early_write(i).wait()
     others = pl.ds(0, GROUP - 1)
     for part in range(PARTS):
         pltpu.make_async_copy(packed.at[part, others], packed.at[part, others], in_send.at[part]).wait()
@@ -428,29 +422,22 @@
             pltpu.make_async_copy(moments.at[part], moments.at[part], note_send.at[part]).wait()
 
 
-def spread(early_hbm, late_hbm, stress, out_hbm, short_hbm, total_hbm, early, late, out, small, sem):
-    loads = [
-        pltpu.make_async_copy(late_hbm.at[pl.ds(16 * i, 16)], late.at[pl.ds(16 * i, 16)], sem.at[i]) for i in range(2)
-    ]
-    loads += [pltpu.make_async_copy(early_hbm.at[i], early.at[i], sem.at[2 + i]) for i in range(2)]
-    for load in loads:
-        load.start()
-    for i in range(2):
-        small[i] = stress[4 * i : 4 * i + 3, :OWN]
+def spread(early, late, stress, out_hbm, short_hbm, total_hbm, out, small, sem):
     copies = [
-        pltpu.make_async_copy(small.at[i], target, sem.at[4 + i]) for i, target in enumerate((short_hbm, total_hbm))
+        pltpu.make_async_copy(early.at[i], out_hbm.at[:, pl.ds(i * 128, 128)], sem.at[i]) for i in range(2)
     ]
     for copy in copies:
         copy.start()
+    for i, target in enumerate((short_hbm, total_hbm)):
+        small[i] = stress[4 * i : 4 * i + 3, :OWN]
+        copies.append(pltpu.make_async_copy(small.at[i], target, sem.at[2 + i]))
+        copies[-1].start()
     for i in range(2):
-        loads[i].wait()
         unpack(late, out.at[i], i)
-        loads[2 + i].wait()
-        for j, source in enumerate((out, early)):
-            columns = pl.ds((256 if j == 0 else 0) + i * 128, 128)
-            copy = pltpu.make_async_copy(source.at[i], out_hbm.at[:, columns], sem.at[6 + 2 * i + j])
-            copy.start()
-            copies.append(copy)
+        copies.append(
+            pltpu.make_async_copy(out.at[i], out_hbm.at[:, pl.ds(256 + i * 128, 128)], sem.at[4 + i])
+        )
+        copies[-1].start()
     for copy in copies:
         copy.wait()
 
@@ -469,12 +456,11 @@
             jax.ShapeDtypeStruct((8, 128), jnp.float32),
         ),
         in_specs=[hbm] * 3,
-        out_specs=(hbm, vmem, vmem),
+        out_specs=(vmem, vmem, vmem),
         scratch_shapes=[
             pltpu.VMEM((4, Q * Q, 128), jnp.float32),
             pltpu.VMEM(velocity.shape, jnp.float32),
             pltpu.VMEM(short_stress.shape, jnp.float32),
-            pltpu.VMEM((2, Q * Q, 128), jnp.float32),
             pltpu.VMEM((GROUP, Q, LANES), jnp.float32),
             pltpu.VMEM((2, 8, 128), jnp.float32),
             pltpu.VMEM(blocks, jnp.float32),
@@ -498,15 +484,15 @@
             dma((4,)),
             dma((PARTS,)),
             dma((2,)),
-            dma((2,)),
         ],
         compiler_params=pltpu.CompilerParams(
             collective_id=0, has_side_effects=True, vmem_limit_bytes=VMEM_LIMIT
         ),
     )(
-        density.reshape(Q * Q, CELLS),
-        velocity,
-        short_stress,
+        *(
+            pltpu.with_memory_space_constraint(one, pltpu.HBM)
+            for one in (density.reshape(Q * Q, CELLS), velocity, short_stress)
+        ),
     )
     result, short_next, total_stress = pl.pallas_call(
         spread,
@@ -516,14 +502,12 @@
             jax.ShapeDtypeStruct(short_stress.shape, jnp.float32),
             jax.ShapeDtypeStruct(short_stress.shape, jnp.float32),
         ),
-        in_specs=[hbm, hbm, vmem],
+        in_specs=[vmem, vmem, vmem],
         out_specs=(hbm, hbm, hbm),
         scratch_shapes=[
             pltpu.VMEM((2, Q * Q, 128), jnp.float32),
-            pltpu.VMEM((GROUP, Q, LANES), jnp.float32),
-            pltpu.VMEM((2, Q * Q, 128), jnp.float32),
             pltpu.VMEM((2,) + short_stress.shape, jnp.float32),
-            dma((10,)),
+            dma((6,)),
         ],
         compiler_params=pltpu.CompilerParams(vmem_limit_bytes=VMEM_LIMIT),
     )(early, late, stress)

time: 112 us -> 109 us (0.973)
  Pallas kernels: 111 us -> 108 us
    pallas_call x1, Pallas kernels: 4.71 us -> 2.79 us  [on_device(): pl.pallas_call(spread, name='spread', out_shape=(jax.ShapeDtypeStruct((Q...]
where the time goes in v3:
time: 109 us
  Pallas kernels  108 us (99%)
    pallas_call x1, Pallas kernels, on_device(): pl.pallas_call(kernel, name='fokker_planck', out_shape=(jax.ShapeDtypeStr...  106 us
    pallas_call x1, Pallas kernels, on_device(): pl.pallas_call(spread, name='spread', out_shape=(jax.ShapeDtypeStruct((Q...  2.79 us

profile of v3, /device:TPU:1, one launch (start us, length us, event | category | flops | bytes accessed | tf_op | source)
XLA Modules:
  0.0 109.0 jit_solution(4432873897208435323)
XLA Ops:
  0.6 105.5 %fokker_planck.1 = (f32[2,1024,128]{2,1,0:T(8,128)S(1)}, f32[32,32,256]{2,1,0:T(8,128)S(1)}, f32[8,128]{1,0:T(8,128)S(1)}) custom-call(f32[1024,512]{1,0:T(8,128)} %bitcast.2, f32[2,2,256]{2,1,0:T(2,128)} %velocity_hbm.1, f32[3,16]{1,0:T(4,128)} %short_hbm.1), custom_call_target="tpu_custom_call" | custom-call | tf_op jit(solution)/shard_map/fokker_planck/pallas_call | solution.py:450
  106.2 2.8 %spread.1 = (f32[1024,512]{1,0:T(8,128)}, f32[3,16]{1,0:T(4,128)}, f32[3,16]{1,0:T(4,128)}) custom-call(f32[2,1024,128]{2,1,0:T(8,128)S(1)} %get-tuple-element.9.early, f32[32,32,256]{2,1,0:T(8,128)S(1)} %get-tuple-element.10.late, f32[8,128]{1,0:T(8,128)S(1)} %get-tuple-element.11.stress), custom_call_target="tpu_custom_call" | custom-call | tf_op jit(solution)/shard_map/spread/pallas_call | solution.py:497

commit v4 on v3

--- a/solution.py
+++ b/solution.py
@@ -107,8 +107,8 @@
         tile, half = turn // 2, turn % 2
         values = [
             arrived[
-                block * 16 + i, pl.ds(pl.multiple_of(tile * TALL, TALL), TALL),
-                pl.ds(pl.multiple_of(half * 128, 128), 128),
+                block * 16 + i, pl.ds(tile * TALL, TALL),
+                pl.ds(half * 128, 128),
             ]
             for i in range(16)
         ]
@@ -117,7 +117,8 @@
             target[pl.ds(tile * (TALL * Q) + half * 16 + i, TALL, stride=Q), :] = values[i]
         return carry
 
-    lax.fori_loop(0, 2 * Q // TALL, piece, 0)
+    for turn in range(2 * Q // TALL):
+        piece(turn, 0)
 
 
 def exact_dot(one, two):
@@ -149,7 +150,7 @@
 def kernel(
     density_hbm, velocity_hbm, short_hbm,
     early, late, stress,
-    density, velocity, short, early_back, inbox, packed, grid, change, spring, wa, wb, wc, halo, lanes, sums, moments,
+    density, velocity, short, early_back, near_back, inbox, packed, grid, change, spring, wa, wb, wc, halo, lanes, sums, moments,
     in_send, in_recv, out_send, out_recv, load_sem, halo_send, halo_recv, read_sem,
     note_send, note_recv,
 ):
@@ -165,18 +166,16 @@
         )
         for i, block in enumerate([2 * (i // 2) + lax.rem(my_y // 2 + i, 2) for i in range(4)])
     ]
-    for read in reads:
-        read.start()
+    reads[0].start()
     barrier = pltpu.get_barrier_semaphore()
 
-    def greet(turn, carry):
+    for turn in range(1, GROUP):
         pl.semaphore_signal(barrier, inc=1, device_id={"conf": lax.rem(me + turn, GROUP)}, device_id_type=MESH)
-        return carry
-
-    lax.fori_loop(1, GROUP, greet, 0)
     for other in (above, below):
         pl.semaphore_signal(barrier, inc=1, device_id={"cell": other}, device_id_type=MESH)
 
+    for read in reads[1:]:
+        read.start()
     loads = [
         pltpu.make_async_copy(source, target, load_sem.at[i])
         for i, (source, target) in enumerate(
@@ -206,12 +205,13 @@
             values = exchange_lanes(values)
             for i in range(16):
                 packed[
-                    part, first * 16 + i, pl.ds(pl.multiple_of(tile * TALL, TALL), TALL),
-                    pl.ds(pl.multiple_of(half * 128, 128), 128),
+                    part, first * 16 + i, pl.ds(tile * TALL, TALL),
+                    pl.ds(half * 128, 128),
                 ] = values[i]
             return carry
 
-        lax.fori_loop(0, 2 * Q // TALL, piece, 0)
+        for turn in range(2 * Q // TALL):
+            piece(turn, 0)
 
     def send_in(part, half):
         def one(turn, carry):
@@ -340,25 +340,30 @@
         for turn in range(STEPS):
             advance(part, turn == STEPS - 1)
 
-        def send_to(arrived):
+        def send_to(arrived, slot, place, turns):
             def send_out(turn, inner):
                 target = peer(turn // 16, lax.rem(turn, 16))
                 pltpu.make_async_remote_copy(
-                    grid.at[part, target], arrived.at[me], out_send.at[part], out_recv.at[part],
+                    grid.at[part, target], arrived.at[place], out_send.at[part], out_recv.at[slot],
                     device_id={"conf": target}, device_id_type=MESH,
                 ).start()
                 return inner
 
-            lax.fori_loop(1, GROUP, send_out, 0)
-            pltpu.make_async_copy(grid.at[part, me], arrived.at[me], out_recv.at[part]).start()
+            lax.fori_loop(*turns, send_out, 0)
+
+        def keep(arrived, slot, place):
+            pltpu.make_async_copy(grid.at[part, me], arrived.at[place], out_recv.at[slot]).start()
 
         @pl.when(part == 0)
         def _():
-            send_to(early_back)
+            send_to(early_back, 0, me, (1, GROUP))
+            keep(early_back, 0, me)
 
         @pl.when(part == 1)
         def _():
-            send_to(late)
+            send_to(near_back, 1, lax.rem(me, 16), (1, 16))
+            send_to(late, 2, lax.rem(me, 16), (16, GROUP))
+            keep(near_back, 1, lax.rem(me, 16))
 
         column = coord(lax.broadcasted_iota(jnp.int32, (Q, 1), 0))
         scale = 1.0 / float(Q**3)
@@ -411,7 +416,9 @@
         return carry
 
     lax.fori_loop(0, 2, early_side, 0)
-    pltpu.make_async_copy(late, late, out_recv.at[1]).wait()
+    pltpu.make_async_copy(near_back, near_back, out_recv.at[1]).wait()
+    unpack(near_back, early.at[2], 0)
+    pltpu.make_async_copy(late, late, out_recv.at[2]).wait()
     others = pl.ds(0, GROUP - 1)
     for part in range(PARTS):
         pltpu.make_async_copy(packed.at[part, others], packed.at[part, others], in_send.at[part]).wait()
@@ -423,21 +430,20 @@
 
 
 def spread(early, late, stress, out_hbm, short_hbm, total_hbm, out, small, sem):
+    near = lax.axis_index("conf") // 16
+    columns = [0, 128] + [pl.multiple_of(place * 128, 128) for place in (2 + near, 3 - near)]
     copies = [
-        pltpu.make_async_copy(early.at[i], out_hbm.at[:, pl.ds(i * 128, 128)], sem.at[i]) for i in range(2)
+        pltpu.make_async_copy(early.at[i], out_hbm.at[:, pl.ds(columns[i], 128)], sem.at[i]) for i in range(3)
     ]
     for copy in copies:
         copy.start()
     for i, target in enumerate((short_hbm, total_hbm)):
         small[i] = stress[4 * i : 4 * i + 3, :OWN]
-        copies.append(pltpu.make_async_copy(small.at[i], target, sem.at[2 + i]))
+        copies.append(pltpu.make_async_copy(small.at[i], target, sem.at[3 + i]))
         copies[-1].start()
-    for i in range(2):
-        unpack(late, out.at[i], i)
-        copies.append(
-            pltpu.make_async_copy(out.at[i], out_hbm.at[:, pl.ds(256 + i * 128, 128)], sem.at[4 + i])
-        )
-        copies[-1].start()
+    unpack(late, out, 0)
+    copies.append(pltpu.make_async_copy(out, out_hbm.at[:, pl.ds(columns[3], 128)], sem.at[5]))
+    copies[-1].start()
     for copy in copies:
         copy.wait()
 
@@ -451,8 +457,8 @@
         kernel,
         name="fokker_planck",
         out_shape=(
-            jax.ShapeDtypeStruct((2, Q * Q, 128), jnp.float32),
-            jax.ShapeDtypeStruct((GROUP, Q, LANES), jnp.float32),
+            jax.ShapeDtypeStruct((3, Q * Q, 128), jnp.float32),
+            jax.ShapeDtypeStruct((GROUP // 2, Q, LANES), jnp.float32),
             jax.ShapeDtypeStruct((8, 128), jnp.float32),
         ),
         in_specs=[hbm] * 3,
@@ -462,6 +468,7 @@
             pltpu.VMEM(velocity.shape, jnp.float32),
             pltpu.VMEM(short_stress.shape, jnp.float32),
             pltpu.VMEM((GROUP, Q, LANES), jnp.float32),
+            pltpu.VMEM((GROUP // 2, Q, LANES), jnp.float32),
             pltpu.VMEM((2, 8, 128), jnp.float32),
             pltpu.VMEM(blocks, jnp.float32),
             pltpu.VMEM(blocks, jnp.float32),
@@ -477,7 +484,7 @@
             dma((PARTS,)),
             dma((PARTS,)),
             dma((PARTS,)),
-            dma((PARTS,)),
+            dma((PARTS + 1,)),
             dma((2,)),
             dma((2,)),
             dma((2,)),
@@ -505,7 +512,7 @@
         in_specs=[vmem, vmem, vmem],
         out_specs=(hbm, hbm, hbm),
         scratch_shapes=[
-            pltpu.VMEM((2, Q * Q, 128), jnp.float32),
+            pltpu.VMEM((Q * Q, 128), jnp.float32),
             pltpu.VMEM((2,) + short_stress.shape, jnp.float32),
             dma((6,)),
         ],

time: 109 us -> 108 us (level)
    pallas_call x1, Pallas kernels: 2.79 us -> 1.59 us  [on_device(): pl.pallas_call(spread, name='spread', out_shape=(jax.ShapeDtypeStruct((Q...]
where the time goes in v4:
time: 108 us
  Pallas kernels  107 us (99%)
    pallas_call x1, Pallas kernels, on_device(): pl.pallas_call(kernel, name='fokker_planck', out_shape=(jax.ShapeDtypeStr...  105 us

profile of v4, /device:TPU:1, one launch (start us, length us, event | category | flops | bytes accessed | tf_op | source)
XLA Modules:
  0.0 107.7 jit_solution(11007379247249723881)
XLA Ops:
  0.6 105.5 %fokker_planck.1 = (f32[3,1024,128]{2,1,0:T(8,128)S(1)}, f32[16,32,256]{2,1,0:T(8,128)S(1)}, f32[8,128]{1,0:T(8,128)S(1)}) custom-call(f32[1024,512]{1,0:T(8,128)} %bitcast.2, f32[2,2,256]{2,1,0:T(2,128)} %velocity_hbm.1, f32[3,16]{1,0:T(4,128)} %short_hbm.1), custom_call_target="tpu_custom_call" | custom-call | tf_op jit(solution)/shard_map/fokker_planck/pallas_call | solution.py:456
  106.1 1.6 %spread.1 = (f32[1024,512]{1,0:T(8,128)}, f32[3,16]{1,0:T(4,128)}, f32[3,16]{1,0:T(4,128)}) custom-call(f32[3,1024,128]{2,1,0:T(8,128)S(1)} %get-tuple-element.9.early, f32[16,32,256]{2,1,0:T(8,128)S(1)} %get-tuple-element.10.late, f32[8,128]{1,0:T(8,128)S(1)} %get-tuple-element.11.stress), custom_call_target="tpu_custom_call" | custom-call | tf_op jit(solution)/shard_map/spread/pallas_call | solution.py:504

commit v5 on v4

--- a/solution.py
+++ b/solution.py
@@ -102,22 +102,22 @@
     return values
 
 
-def unpack(arrived, target, block):
+def unpack(arrived, target, block, tall=TALL, first=0, last=2 * Q // TALL):
     def piece(turn, carry):
         tile, half = turn // 2, turn % 2
         values = [
             arrived[
-                block * 16 + i, pl.ds(tile * TALL, TALL),
+                block * 16 + i, pl.ds(tile * tall, tall),
                 pl.ds(half * 128, 128),
             ]
             for i in range(16)
         ]
         values = exchange_lanes(values)
         for i in range(16):
-            target[pl.ds(tile * (TALL * Q) + half * 16 + i, TALL, stride=Q), :] = values[i]
+            target[pl.ds(tile * (tall * Q) + half * 16 + i, tall, stride=Q), :] = values[i]
         return carry
 
-    for turn in range(2 * Q // TALL):
+    for turn in range(first, last):
         piece(turn, 0)
 
 
@@ -169,8 +169,12 @@
     reads[0].start()
     barrier = pltpu.get_barrier_semaphore()
 
-    for turn in range(1, GROUP):
-        pl.semaphore_signal(barrier, inc=1, device_id={"conf": lax.rem(me + turn, GROUP)}, device_id_type=MESH)
+    for turn in sorted(range(1, GROUP), key=lambda turn: -(turn // 2 % 4 == 2) - (turn // 2 % 4 > 0)):
+        pl.semaphore_signal(
+            barrier, inc=1,
+            device_id={"conf": lax.rem(my_y + turn // 8, 4) * 8 + lax.rem(my_z + turn // 2, 4) * 2 + lax.rem(my_c + turn, 2)},
+            device_id_type=MESH,
+        )
     for other in (above, below):
         pl.semaphore_signal(barrier, inc=1, device_id={"cell": other}, device_id_type=MESH)
 
@@ -222,11 +226,13 @@
             ).start()
             return carry
 
-        lax.fori_loop(jnp.where(half == 0, 1, 0), 16, one, 0)
+        for turn in range(1 if half == 0 else 0, 16):
+            one(turn, 0)
 
     reads[0].wait()
     pack(0, 0)
     pl.semaphore_wait(barrier, GROUP + 1)
+    send_in(0, 0)
     loads[0].wait()
     to_above = pltpu.make_async_remote_copy(
         velocity, halo.at[1], halo_send.at[0], halo_recv.at[1], device_id={"cell": above}, device_id_type=MESH
@@ -236,11 +242,10 @@
     )
     to_above.start()
     to_below.start()
-    send_in(0, jnp.int32(0))
     for i in range(1, 4):
         reads[i].wait()
         pack(i // 2, i % 2)
-        send_in(i // 2, jnp.int32(i % 2))
+        send_in(i // 2, i % 2)
     for part in range(PARTS):
         pltpu.make_async_copy(packed.at[part, me], grid.at[part, me], in_recv.at[part]).start()
 
@@ -441,9 +446,11 @@
         small[i] = stress[4 * i : 4 * i + 3, :OWN]
         copies.append(pltpu.make_async_copy(small.at[i], target, sem.at[3 + i]))
         copies[-1].start()
-    unpack(late, out, 0)
-    copies.append(pltpu.make_async_copy(out, out_hbm.at[:, pl.ds(columns[3], 128)], sem.at[5]))
-    copies[-1].start()
+    for i in range(2):
+        unpack(late, out, 0, Q // 2, 2 * i, 2 * i + 2)
+        rows = pl.ds(i * (Q * Q // 2), Q * Q // 2)
+        copies.append(pltpu.make_async_copy(out.at[rows], out_hbm.at[rows, pl.ds(columns[3], 128)], sem.at[5 + i]))
+        copies[-1].start()
     for copy in copies:
         copy.wait()
 
@@ -514,7 +521,7 @@
         scratch_shapes=[
             pltpu.VMEM((Q * Q, 128), jnp.float32),
             pltpu.VMEM((2,) + short_stress.shape, jnp.float32),
-            dma((6,)),
+            dma((7,)),
         ],
         compiler_params=pltpu.CompilerParams(vmem_limit_bytes=VMEM_LIMIT),
     )(early, late, stress)

time: 108 us -> 108 us (level)
  no operation moved by 1% of the time
where the time goes in v5:
time: 108 us
  Pallas kernels  107 us (99%)
    pallas_call x1, Pallas kernels, on_device(): pl.pallas_call(kernel, name='fokker_planck', out_shape=(jax.ShapeDtypeStr...  105 us

profile of v5, /device:TPU:1, one launch (start us, length us, event | category | flops | bytes accessed | tf_op | source)
XLA Modules:
  0.0 107.6 jit_solution(16690742923961394132)
XLA Ops:
  0.6 105.4 %fokker_planck.1 = (f32[3,1024,128]{2,1,0:T(8,128)S(1)}, f32[16,32,256]{2,1,0:T(8,128)S(1)}, f32[8,128]{1,0:T(8,128)S(1)}) custom-call(f32[1024,512]{1,0:T(8,128)} %bitcast.2, f32[2,2,256]{2,1,0:T(2,128)} %velocity_hbm.1, f32[3,16]{1,0:T(4,128)} %short_hbm.1), custom_call_target="tpu_custom_call" | custom-call | tf_op jit(solution)/shard_map/fokker_planck/pallas_call | solution.py:463
  106.0 1.6 %spread.1 = (f32[1024,512]{1,0:T(8,128)}, f32[3,16]{1,0:T(4,128)}, f32[3,16]{1,0:T(4,128)}) custom-call(f32[3,1024,128]{2,1,0:T(8,128)S(1)} %get-tuple-element.9.early, f32[16,32,256]{2,1,0:T(8,128)S(1)} %get-tuple-element.10.late, f32[8,128]{1,0:T(8,128)S(1)} %get-tuple-element.11.stress), custom_call_target="tpu_custom_call" | custom-call | tf_op jit(solution)/shard_map/spread/pallas_call | solution.py:511
